TPU v7x, 512 devices: a whole 4x4x16 slice. The times are simulated.
512 devices in a mesh: gz: 64 (over z, x), gx: 4 (over y_lo, core), gy: 2 (over y_hi).
Axes of the slice: x: 4, y: 4 (y_hi: 2, y_lo: 2; y = y_hi * 2 + y_lo), z: 16, core: 2. Of those that a mesh axis runs over, the one named last changes fastest.
Arguments:
- populations: float32 [19, 64, 256, 256], P(None, 'gz', 'gx', 'gy'), as said below
- solid_mask: int32 [64, 256, 256], P('gz', 'gx', 'gy'), may hold values from 0 to 1, as said below
- whirl_offsets: int32 [3, 2], replicated, may hold values from -3 to 3
- marker_cells: int32 [2, 64, 256], P(None, 'gz', ('gx', 'gy')), may hold values from -33 to 33, as said below
- marker_weights: float32 [2, 4, 64, 256], P(None, None, 'gz', ('gx', 'gy')), as said below
- pipe_velocity: float32 [3, 64, 256], P(None, 'gz', ('gx', 'gy')), may hold values from -0.2 to 0.2
Outputs:
- new_populations: float32 [19, 64, 256, 256], P(None, 'gz', 'gx', 'gy')
- velocity_field: float32 [3, 64, 256, 256], P(None, 'gz', 'gx', 'gy')
- marker_force: float32 [3, 64, 256], P(None, 'gz', ('gx', 'gy'))
Inputs may be any that keep to these rules, and one draw needn't show every extreme that they name: `solid_mask`: 1 marks cells of the casing wall and of cuttings stuck to it; every cell on the grid's faces along the first and second cross-section dimensions is solid, and every cell within 38 cells of the grid's centre line along both is mud. `marker_cells`: every cycle traces the same octagon of radius 32 cells around the pipe axis, shifted by -1, 0 or 1 cell along each cross-section dimension, the same for all markers of a cycle. `marker_weights`: nonnegative kernel weights. `populations`: positive values near 1/3, 1/18 and 1/36 times a density near 1.
All inputs are finite; a program needn't handle non-finite values.
Results may differ from a plain program's by a relative error of at most 0.0003.
Values sent between devices are 32-bit elements; how exact they have to be, the bound alone decides.
A program may use at most 64 MiB of HBM per device.

v0:
```python
import functools

import jax
import jax.numpy as jnp
from jax import lax
from jax.experimental import pallas as pl
from jax.experimental.pallas import tpu as pltpu
from jax.sharding import PartitionSpec as P

MESH = pl.DeviceIdType.MESH
STEPS = 3
RELAX_TIME = 0.8
SPEED_SCALE = 0.05

VELOCITIES = [
    (0, 0, 0),
    (1, 0, 0),
    (-1, 0, 0),
    (0, 1, 0),
    (0, -1, 0),
    (0, 0, 1),
    (0, 0, -1),
    (1, 1, 0),
    (-1, -1, 0),
    (1, -1, 0),
    (-1, 1, 0),
    (1, 0, 1),
    (-1, 0, -1),
    (1, 0, -1),
    (-1, 0, 1),
    (0, 1, 1),
    (0, -1, -1),
    (0, 1, -1),
    (0, -1, 1),
]
INDEX = {vector: member for member, vector in enumerate(VELOCITIES)}
INPLANE = [
    (0, 0, 0),
    (0, 0, 1),
    (0, 0, -1),
    (0, 1, 0),
    (0, 1, 1),
    (0, 1, -1),
    (0, -1, 0),
    (0, -1, 1),
    (0, -1, -1),
]
AXIAL = [
    [(1, 0, 0), (1, 0, 1), (1, 0, -1), (1, 1, 0), (1, -1, 0)],
    [(-1, 0, 0), (-1, 0, 1), (-1, 0, -1), (-1, 1, 0), (-1, -1, 0)],
]
EDGES = [
    (0, 0, 1),
    (0, 0, -1),
    (0, 1, 1),
    (0, 1, -1),
    (0, -1, 1),
    (0, -1, -1),
    (1, 0, 1),
    (1, 0, -1),
    (-1, 0, 1),
    (-1, 0, -1),
]
DIAGONAL = [(0, 1, 1), (0, 1, -1), (0, -1, 1), (0, -1, -1)]

BLOCKS = 8
OUTER_BLOCKS = 3
OUTER_ROWS = 24
CENTRE_ROWS = 40
N_AXIAL = 0
N_AXIAL_ROW = 4
N_ROW = 8
N_EDGE = 10
N_SAMPLE = 15
N_MESSAGES = 24


def tree_sum(values):
    while len(values) > 1:
        pairs = [values[i] + values[i + 1] for i in range(0, len(values) - 1, 2)]
        if len(values) % 2:
            pairs.append(values[-1])
        values = pairs
    return values[0]


def moments(f):
    density = tree_sum(f)
    inverse = 1.0 / density
    components = []
    for column in range(3):
        ahead = tree_sum([f[m] for m in range(19) if VELOCITIES[m][column] == 1])
        back = tree_sum([f[m] for m in range(19) if VELOCITIES[m][column] == -1])
        components.append((ahead - back) * inverse)
    return density, inverse, components


def dot(vector, u):
    total = None
    for c, x in zip(vector, u):
        if c == 0:
            continue
        if total is None:
            total = x if c == 1 else -x
        else:
            total = total + x if c == 1 else total - x
    return total


def collide(f, density, u, fluid):
    base = 1.0 - 1.5 * (u[0] * u[0] + u[1] * u[1] + u[2] * u[2])
    keep = 1.0 - 1.0 / RELAX_TIME
    scaled = density * (1.0 / RELAX_TIME)
    heavy = scaled * (1.0 / 18.0)
    light = scaled * (1.0 / 36.0)
    post = [None] * 19
    post[0] = jnp.where(fluid, scaled * (1.0 / 3.0) * base + keep * f[0], f[0])
    for m in range(1, 19, 2):
        weight = heavy if m < 7 else light
        projected = dot(VELOCITIES[m], u)
        even = weight * (base + 4.5 * (projected * projected))
        odd = (3.0 * weight) * projected
        post[m] = jnp.where(fluid, (even + odd) + keep * f[m], f[m + 1])
        post[m + 1] = jnp.where(fluid, (even - odd) + keep * f[m + 1], f[m])
    return post


def split(x):
    high = x.astype(jnp.bfloat16)
    low = (x - high.astype(jnp.float32)).astype(jnp.bfloat16)
    return high, low


def product(x, w_high, w_low, dims):
    high, low = split(x)
    one = functools.partial(
        lax.dot_general, dimension_numbers=(dims, ((), ())), preferred_element_type=jnp.float32
    )
    return one(high, w_high) + (one(low, w_high) + one(high, w_low))


def kernel(
    gz_size,
    pops,
    solid,
    whirl,
    cells,
    weights,
    target,
    out_pops,
    out_vel,
    out_force,
    pb,
    zs,
    zr,
    es,
    er,
    pp,
    st,
    mom,
    fb,
    mk_own,
    mk_all,
    mk,
    sp,
    wx,
    wy_high,
    wy_low,
    send_sem,
    recv_sem,
    mk_send,
    mk_recv,
):
    gz = lax.axis_index("gz")
    gx = lax.axis_index("gx")
    gy = lax.axis_index("gy")
    z_next, z_prev = lax.rem(gz + 1, gz_size), lax.rem(gz + gz_size - 1, gz_size)
    x_next, x_prev, x_far = lax.rem(gx + 1, 4), lax.rem(gx + 3, 4), lax.rem(gx + 2, 4)
    y_other = 1 - gy
    flip = gx // 2
    is_centre = lax.rem((gx + 1) // 2, 2)
    centre = is_centre == 1
    outer = is_centre == 0
    quarter = lax.rem(2 * gx + gy + 2, 4)
    own = 2 * gx + gy
    outer_start = pl.multiple_of(40 * flip, 8)
    centre_start = pl.multiple_of(24 * (1 - flip), 8)

    barrier = pltpu.get_barrier_semaphore()
    neighbours = [
        {"gz": gz, "gx": x_next, "gy": gy},
        {"gz": gz, "gx": x_prev, "gy": gy},
        {"gz": gz, "gx": x_far, "gy": gy},
        {"gz": gz, "gx": gx, "gy": y_other},
        {"gz": gz, "gx": x_next, "gy": y_other},
        {"gz": gz, "gx": x_prev, "gy": y_other},
        {"gz": gz, "gx": x_far, "gy": y_other},
    ]
    for z in (z_next, z_prev):
        neighbours += [
            {"gz": z, "gx": gx, "gy": gy},
            {"gz": z, "gx": x_next, "gy": gy},
            {"gz": z, "gx": x_prev, "gy": gy},
            {"gz": z, "gx": gx, "gy": y_other},
        ]
    for place in neighbours:
        pl.semaphore_signal(barrier, inc=1, device_id=place, device_id_type=MESH)

    lane = lax.broadcasted_iota(jnp.int32, (8, 128), 1)
    lane_block = lane // 16

    def block_of(b):
        return b + flip * (BLOCKS - 1 - 2 * b)

    def remote(src, dst, s, n, place, n_recv=None):
        return pltpu.make_async_remote_copy(
            src_ref=src,
            dst_ref=dst,
            send_sem=send_sem.at[s, n],
            recv_sem=recv_sem.at[s, n if n_recv is None else n_recv],
            device_id=place,
            device_id_type=MESH,
        )

    def axial(s, way, part):
        start, size = ((outer_start, OUTER_ROWS), (centre_start, CENTRE_ROWS))[part]
        return remote(
            zs.at[s, way, :, pl.ds(start, size), :],
            zr.at[s, way, :, pl.ds(pl.multiple_of(start + 8, 8), size), :],
            s,
            N_AXIAL + 2 * way + part,
            {"gz": (z_next, z_prev)[way], "gx": gx, "gy": gy},
        )

    def small(s):
        copies = []
        for way in range(2):
            z = (z_next, z_prev)[way]
            copies.append(
                remote(
                    zs.at[s, way, 3, pl.ds(56, 8), :],
                    zr.at[s, way, 3, pl.ds(0, 8), :],
                    s,
                    N_AXIAL_ROW + 2 * way,
                    {"gz": z, "gx": x_next, "gy": gy},
                )
            )
            copies.append(
                remote(
                    zs.at[s, way, 4, pl.ds(0, 8), :],
                    zr.at[s, way, 4, pl.ds(72, 8), :],
                    s,
                    N_AXIAL_ROW + 2 * way + 1,
                    {"gz": z, "gx": x_prev, "gy": gy},
                )
            )
        copies.append(
            remote(
                pb.at[s, pl.ds(3, 3), pl.ds(64, 8), :],
                pb.at[s, pl.ds(3, 3), pl.ds(0, 8), :],
                s,
                N_ROW,
                {"gz": gz, "gx": x_next, "gy": gy},
            )
        )
        copies.append(
            remote(
                pb.at[s, pl.ds(6, 3), pl.ds(8, 8), :],
                pb.at[s, pl.ds(6, 3), pl.ds(72, 8), :],
                s,
                N_ROW + 1,
                {"gz": gz, "gx": x_prev, "gy": gy},
            )
        )
        places = [
            {"gz": gz, "gx": gx, "gy": y_other},
            {"gz": gz, "gx": x_next, "gy": y_other},
            {"gz": gz, "gx": x_prev, "gy": y_other},
            {"gz": z_next, "gx": gx, "gy": y_other},
            {"gz": z_prev, "gx": gx, "gy": y_other},
        ]
        for k, place in enumerate(places):
            copies.append(remote(es.at[s], er.at[s, k], s, N_EDGE + k, place))
        return copies

    def sample_copies(s):
        pair = 3 - gx
        places = [(gx, y_other), (pair, gy), (pair, y_other)]
        if s == STEPS - 1:
            places += [(0, gy), (0, y_other), (3, gy), (3, y_other)]
        return [
            remote(
                sp.at[s, quarter],
                sp.at[s, quarter],
                s,
                N_SAMPLE + d,
                {"gz": gz, "gx": x, "gy": y},
                N_SAMPLE + quarter,
            )
            for d, (x, y) in enumerate(places)
        ]

    def sample_wait(s, q):
        remote(sp.at[s, q], sp.at[s, q], s, N_SAMPLE, neighbours[0], N_SAMPLE + q).wait_recv()

    def centre_place(t):
        return {"gz": gz, "gx": 1 + t // 2, "gy": t % 2}

    def marker_copy(t):
        return pltpu.make_async_remote_copy(
            src_ref=mk_all.at[own],
            dst_ref=mk_all.at[own],
            send_sem=mk_send.at[t],
            recv_sem=mk_recv.at[own],
            device_id=centre_place(t),
            device_id_type=MESH,
        )

    def marker_wait(j):
        pltpu.make_async_remote_copy(
            src_ref=mk_all.at[j],
            dst_ref=mk_all.at[j],
            send_sem=mk_send.at[0],
            recv_sem=mk_recv.at[j],
            device_id=neighbours[0],
            device_id_type=MESH,
        ).wait_recv()

    def not_self(t):
        return jnp.logical_or(gx != 1 + t // 2, gy != t % 2)

    def edge(value, packed, vector):
        j = EDGES.index(vector)
        if vector[2] == 1:
            there = packed if j == 0 else pltpu.roll(packed, 128 - j, 1)
            return jnp.where(lane == 0, there, value)
        return jnp.where(lane == 127, pltpu.roll(packed, 127 - j, 1), value)

    def gather(s, rb):
        row = pl.multiple_of(rb * 8, 8)
        if s == 0:
            return [pops[m, 0, pl.ds(row, 8), :] for m in range(19)]
        back = lax.rem(128 - 16 * rb, 128)
        packed = {
            0: pltpu.roll(er[s - 1, 0], back, 1),
            1: pltpu.roll(er[s - 1, 3], back, 1),
            -1: pltpu.roll(er[s - 1, 4], back, 1),
        }
        f = []
        for vector in VELOCITIES:
            rows = pl.ds(row + (8 - vector[1]), 8)
            if vector in DIAGONAL:
                f.append(pp[DIAGONAL.index(vector), rows, :])
                continue
            if vector[0] == 0:
                value = pb[s - 1, INPLANE.index(vector), rows, :]
            else:
                way = 0 if vector[0] == 1 else 1
                value = zr[s - 1, way, AXIAL[way].index(vector), rows, :]
            if vector[2] != 0:
                value = edge(value, packed[vector[0]], vector)
            f.append(value)
        return f

    def patch(s):
        def block(rb, carry):
            row = pl.multiple_of(rb * 8 + 8, 8)
            packed = pltpu.roll(er[s - 1, 0], lax.rem(128 - 16 * rb, 128), 1)
            for k, vector in enumerate(DIAGONAL):
                value = pb[s - 1, INPLANE.index(vector), pl.ds(row, 8), :]
                pp[k, pl.ds(row, 8), :] = edge(value, packed, vector)
            return carry

        lax.fori_loop(0, BLOCKS, block, 0)
        before = pltpu.roll(er[s - 1, 1], 16, 1)
        after = er[s - 1, 2]
        for k, vector in enumerate(DIAGONAL):
            packed, row = (before, 0) if vector[1] == 1 else (after, 72)
            value = pb[s - 1, INPLANE.index(vector), pl.ds(row, 8), :]
            pp[k, pl.ds(row, 8), :] = edge(value, packed, vector)

    def store_post(s, rb, post):
        row = pl.multiple_of(rb * 8, 8)
        for vector in VELOCITIES:
            value = post[INDEX[vector]]
            if vector[2] != 0:
                value = pltpu.roll(value, 1 if vector[2] == 1 else 127, 1)
            if vector[0] == 0:
                pb[s, INPLANE.index(vector), pl.ds(pl.multiple_of(row + 8, 8), 8), :] = value
            else:
                way = 0 if vector[0] == 1 else 1
                zs[s, way, AXIAL[way].index(vector), pl.ds(row, 8), :] = value
        packed = post[INDEX[EDGES[0]]]
        packed = pltpu.roll(packed, 1, 1)
        for j, vector in enumerate(EDGES):
            if j == 0:
                continue
            shift = j + 1 if vector[2] == 1 else j
            packed = jnp.where(lane == j, pltpu.roll(post[INDEX[vector]], shift, 1), packed)
        es[s] = jnp.where(lane_block == rb, pltpu.roll(packed, 16 * rb, 1), es[s])

    def fluid_of(rb):
        return solid[0, pl.ds(pl.multiple_of(rb * 8, 8), 8), :] == 0

    def whole_block(s):
        def block(b, carry):
            rb = block_of(b)
            f = gather(s, rb)
            density, _, u = moments(f)
            store_post(s, rb, collide(f, density, u, fluid_of(rb)))
            return carry

        return block

    def first_half(s):
        def block(b, carry):
            rb = block_of(b)
            row = pl.multiple_of(rb * 8, 8)
            f = gather(s, rb)
            density, inverse, u = moments(f)
            if s > 0:
                for m in range(19):
                    st[m, pl.ds(row, 8), :] = f[m]
            for c, value in enumerate([*u, density, inverse]):
                mom[c, pl.ds(row, 8), :] = value
            return carry

        return block

    def second_half(s):
        def block(b, carry):
            rb = block_of(b)
            row = pl.multiple_of(rb * 8, 8)
            if s == 0:
                f = [pops[m, 0, pl.ds(row, 8), :] for m in range(19)]
            else:
                f = [st[m, pl.ds(row, 8), :] for m in range(19)]
            density = mom[3, pl.ds(row, 8), :]
            scale = RELAX_TIME * mom[4, pl.ds(row, 8), :]
            near = pl.multiple_of(row - centre_start, 8)
            u = [mom[c, pl.ds(row, 8), :] + scale * fb[c, pl.ds(near, 8), :] for c in range(3)]
            store_post(s, rb, collide(f, density, u, fluid_of(rb)))
            return carry

        return block

    def marker_matrices(s):
        def matrix(size, first, base, row):
            place = lax.broadcasted_iota(jnp.int32, (size, 256), 0) + first
            distance = place.astype(jnp.float32) - base
            result = jnp.zeros((size, 256), jnp.float32)
            for a in range(4):
                result = jnp.where(distance == float(a), mk[row + a : row + a + 1, :], result)
            return result

        base_x = mk[0:1, :] + (127 + whirl[s, 0]).astype(jnp.float32)
        base_y = mk[1:2, :] + (127 + whirl[s, 1]).astype(jnp.float32)
        wx[...] = matrix(CENTRE_ROWS, 64 * gx + centre_start, base_x, 2)
        high, low = split(matrix(128, 128 * gy, base_y, 6))
        wy_high[...] = high
        wy_low[...] = low

    def sample(s):
        u = mom[0:3, pl.ds(centre_start, CENTRE_ROWS), :].reshape(3 * CENTRE_ROWS, 128)
        along = product(u, wy_high[...], wy_low[...], ((1,), (0,)))
        spread = wx[...]
        rows = [
            jnp.sum(along[c * CENTRE_ROWS : (c + 1) * CENTRE_ROWS] * spread, axis=0, keepdims=True)
            for c in range(3)
        ]
        sp[s, quarter] = jnp.concatenate(rows + [jnp.zeros((5, 256), jnp.float32)], axis=0)

    def sampled(s):
        return (sp[s, 0] + sp[s, 1]) + (sp[s, 2] + sp[s, 3])

    def force(s):
        push = mk[10:13, :] - sampled(s)[0:3, :]
        spread = wx[...]
        weighted = jnp.concatenate([spread * push[c : c + 1, :] for c in range(3)], axis=0)
        body = product(weighted, wy_high[...], wy_low[...], ((1,), (1,)))
        fb[...] = body.reshape(3, CENTRE_ROWS, 128)

    mk_own[...] = jnp.zeros((16, 128), jnp.float32)
    mk_own[0:2, 0:32] = cells[:, 0, :].astype(jnp.float32)
    mk_own[2:6, 0:32] = weights[0, :, 0, :]
    mk_own[6:10, 0:32] = weights[1, :, 0, :]
    mk_own[10:13, 0:32] = target[:, 0, :]
    mk_all[own] = pltpu.roll(mk_own[...], 32 * lax.rem(own, 4), 1)

    pl.semaphore_wait(barrier, len(neighbours))

    for t in range(4):

        @pl.when(not_self(t))
        def _(t=t):
            marker_copy(t).start()

    for s in range(STEPS):
        last = s == STEPS - 1
        if s > 0:
            for copy in [axial(s - 1, way, part) for way in range(2) for part in range(2)] + small(s - 1):
                copy.wait_recv()
            patch(s)

        @pl.when(centre)
        def _(s=s):
            lax.fori_loop(OUTER_BLOCKS, BLOCKS, first_half(s), 0)
            if s == 0:
                for d in range(1, 8):
                    marker_wait(lax.rem(own + d, 8))
                mk[:, 0:128] = (mk_all[0] + mk_all[1]) + (mk_all[2] + mk_all[3])
                mk[:, 128:256] = (mk_all[4] + mk_all[5]) + (mk_all[6] + mk_all[7])
                marker_matrices(s)
            sample(s)
            for copy in sample_copies(s):
                copy.start()

        lax.fori_loop(0, OUTER_BLOCKS, whole_block(s), 0)
        for way in range(2):
            axial(s, way, 0).start()

        @pl.when(outer)
        def _(s=s):
            lax.fori_loop(OUTER_BLOCKS, BLOCKS, whole_block(s), 0)

        @pl.when(centre)
        def _(s=s):
            for d in range(1, 4):
                sample_wait(s, lax.rem(quarter + d, 4))
            force(s)
            lax.fori_loop(OUTER_BLOCKS, BLOCKS, second_half(s), 0)

        for way in range(2):
            axial(s, way, 1).start()
        for copy in small(s):
            copy.start()

        if not last:

            @pl.when(centre)
            def _(s=s):
                marker_matrices(s + 1)

    for copy in [axial(STEPS - 1, way, part) for way in range(2) for part in range(2)] + small(STEPS - 1):
        copy.wait_recv()
    patch(STEPS)

    def final_block(rb, carry):
        rows = pl.ds(pl.multiple_of(rb * 8, 8), 8)
        f = gather(STEPS, rb)
        for m in range(19):
            out_pops[m, 0, rows, :] = f[m]
        _, _, u = moments(f)
        fluid = fluid_of(rb)
        for c in range(3):
            out_vel[c, 0, rows, :] = jnp.where(fluid, u[c] * (1.0 / SPEED_SCALE), 0.0)
        return carry

    lax.fori_loop(0, BLOCKS, final_block, 0)

    @pl.when(outer)
    def _():
        for q in range(4):
            sample_wait(STEPS - 1, q)

    total = sampled(STEPS - 1)
    half = jnp.where(own // 4 == 0, total[:, 0:128], total[:, 128:256])
    half = pltpu.roll(half, lax.rem(128 - 32 * lax.rem(own, 4), 128), 1)
    out_force[:, 0, :] = (target[:, 0, :] - half[0:3, 0:32]) * (1.0 / SPEED_SCALE)

    for t in range(4):

        @pl.when(not_self(t))
        def _(t=t):
            marker_copy(t).wait_send()

    for s in range(STEPS):
        for copy in [axial(s, way, part) for way in range(2) for part in range(2)] + small(s):
            copy.wait_send()

    @pl.when(centre)
    def _():
        for s in range(STEPS):
            for copy in sample_copies(s):
                copy.wait_send()


def body(populations, solid_mask, whirl_offsets, marker_cells, marker_weights, pipe_velocity):
    f32 = jnp.float32
    vmem = pl.BlockSpec(memory_space=pltpu.VMEM)
    return pl.pallas_call(
        functools.partial(kernel, lax.axis_size("gz")),
        out_shape=(
            jax.ShapeDtypeStruct(populations.shape, f32),
            jax.ShapeDtypeStruct((3,) + solid_mask.shape, f32),
            jax.ShapeDtypeStruct(pipe_velocity.shape, f32),
        ),
        in_specs=[vmem, vmem, pl.BlockSpec(memory_space=pltpu.SMEM), vmem, vmem, vmem],
        out_specs=(vmem, vmem, vmem),
        scratch_shapes=[
            pltpu.VMEM((STEPS, 9, 80, 128), f32),
            pltpu.VMEM((STEPS, 2, 5, 64, 128), f32),
            pltpu.VMEM((STEPS, 2, 5, 80, 128), f32),
            pltpu.VMEM((STEPS, 8, 128), f32),
            pltpu.VMEM((STEPS, 5, 8, 128), f32),
            pltpu.VMEM((4, 80, 128), f32),
            pltpu.VMEM((19, 64, 128), f32),
            pltpu.VMEM((5, 64, 128), f32),
            pltpu.VMEM((3, CENTRE_ROWS, 128), f32),
            pltpu.VMEM((16, 128), f32),
            pltpu.VMEM((8, 16, 128), f32),
            pltpu.VMEM((16, 256), f32),
            pltpu.VMEM((STEPS, 4, 8, 256), f32),
            pltpu.VMEM((CENTRE_ROWS, 256), f32),
            pltpu.VMEM((128, 256), jnp.bfloat16),
            pltpu.VMEM((128, 256), jnp.bfloat16),
            pltpu.SemaphoreType.DMA((STEPS, N_MESSAGES)),
            pltpu.SemaphoreType.DMA((STEPS, N_MESSAGES)),
            pltpu.SemaphoreType.DMA((4,)),
            pltpu.SemaphoreType.DMA((8,)),
        ],
        compiler_params=pltpu.CompilerParams(
            collective_id=0, has_side_effects=True, vmem_limit_bytes=24 * 1024 * 1024
        ),
        cost_estimate=pl.CostEstimate(flops=40_000_000, bytes_accessed=2_000_000, transcendentals=0),
    )(populations, solid_mask, whirl_offsets, marker_cells, marker_weights, pipe_velocity)


def solution(mesh):
    in_specs = (
        P(None, "gz", "gx", "gy"),
        P("gz", "gx", "gy"),
        P(),
        P(None, "gz", ("gx", "gy")),
        P(None, None, "gz", ("gx", "gy")),
        P(None, "gz", ("gx", "gy")),
    )
    out_specs = (P(None, "gz", "gx", "gy"), P(None, "gz", "gx", "gy"), P(None, "gz", ("gx", "gy")))
    return jax.shard_map(body, mesh=mesh, in_specs=in_specs, out_specs=out_specs, check_vma=False)
```

profile of v0, /device:TPU:1, one launch (start us, length us, event | category | flops | bytes accessed | tf_op | source)
XLA Modules:
  0.0 65.0 jit_solution(10238994683392601695)
XLA Ops:
  0.6 0.0 copy-start.3
  0.6 0.0 copy-start.4
  0.7 0.8 %copy.9.whirl = s32[3,2]{1,0:T(4,128)S(1)} copy(s32[3,2]{0,1:T(2,128)} %param.8) | data formatting | bytes 48 | tf_op args[2]
  1.4 0.0 copy-done.3
  1.4 0.0 copy-done.4
  1.4 0.0 copy-start
  1.4 1.1 %copy-done = f32[19,1,64,128]{3,2,1,0:T(8,128)S(1)} copy-done((f32[19,1,64,128]{3,2,1,0:T(8,128)S(1)}, f32[19,1,64,128]{3,2,1,0:T(8,128)}, u32[]{:S(2)}) %copy-start) | copy-done | bytes 622616
  2.5 0.0 copy-start.1
  2.5 0.8 %copy-done.1 = s32[1,64,128]{2,1,0:T(8,128)S(1)} copy-done((s32[1,64,128]{2,1,0:T(8,128)S(1)}, s32[1,64,128]{2,1,0:T(8,128)}, u32[]{:S(2)}) %copy-start.1) | copy-done | bytes 32792
  3.3 0.0 copy-start.2
  3.3 0.7 %copy-done.2 = f32[2,4,1,32]{3,2,1,0:T(1,128)S(1)} copy-done((f32[2,4,1,32]{3,2,1,0:T(1,128)S(1)}, f32[2,4,1,32]{3,2,1,0:T(1,128)}, u32[]{:S(2)}) %copy-start.2) | copy-done | bytes 1048
  4.0 59.0 %shard_map.85 = (f32[19,1,64,128]{3,2,1,0:T(8,128)S(1)}, f32[3,1,64,128]{3,2,1,0:T(8,128)S(1)}, f32[3,1,32]{2,1,0:T(1,128)S(1)}) custom-call(f32[19,1,64,128]{3,2,1,0:T(8,128)S(1)} %copy-done, s32[1,64,128]{2,1,0:T(8,128)S(1)} %copy-done.1, s32[3,2]{1,0:T(4,128)S(1)} %copy.9.whirl, s32[2,1,32]{2,1,0:T(1,128)S(1)} %copy-done.4, ...), custom_call_target="tpu_custom_call" | custom-call | flops 40000000 | bytes 2000000 | tf_op jit(solution)/shard_map/pallas_call | solution.py:591
  62.9 0.8 %copy.13 = f32[19,1,64,128]{3,2,1,0:T(8,128)} copy(f32[19,1,64,128]{3,2,1,0:T(8,128)S(1)} %get-tuple-element.6) | data formatting | bytes 1245184
  63.8 0.6 copy.14
  64.4 0.6 copy.15
Async XLA Ops:
  0.6 0.8 %copy-start.3 = (f32[3,1,32]{2,1,0:T(1,128)S(1)}, f32[3,1,32]{2,1,0:T(1,128)}, u32[]{:S(2)}) copy-start(f32[3,1,32]{2,1,0:T(1,128)} %target.1) | copy-start | bytes 1156
  0.6 0.8 %copy-start.4 = (s32[2,1,32]{2,1,0:T(1,128)S(1)}, s32[2,1,32]{2,1,0:T(1,128)}, u32[]{:S(2)}) copy-start(s32[2,1,32]{2,1,0:T(1,128)} %cells.1) | copy-start | bytes 772
  1.4 1.1 %copy-start = (f32[19,1,64,128]{3,2,1,0:T(8,128)S(1)}, f32[19,1,64,128]{3,2,1,0:T(8,128)}, u32[]{:S(2)}) copy-start(f32[19,1,64,128]{3,2,1,0:T(8,128)} %pops.1) | copy-start | bytes 1867780
  2.5 0.8 %copy-start.1 = (s32[1,64,128]{2,1,0:T(8,128)S(1)}, s32[1,64,128]{2,1,0:T(8,128)}, u32[]{:S(2)}) copy-start(s32[1,64,128]{2,1,0:T(8,128)} %solid.1) | copy-start | bytes 98308
  3.3 0.7 %copy-start.2 = (f32[2,4,1,32]{3,2,1,0:T(1,128)S(1)}, f32[2,4,1,32]{3,2,1,0:T(1,128)}, u32[]{:S(2)}) copy-start(f32[2,4,1,32]{3,2,1,0:T(1,128)} %weights.1) | copy-start | bytes 3076
where the time goes:
time: 65.3 us; the launch traced here: 65 us
  Pallas kernels  59 us (90%)
  local copies, waits for them, and re-layouts  5.34 us (8%)
  between operations  0.66 us (1%)
    pallas_call x1, Pallas kernels, body(): pl.pallas_call(functools.partial(kernel, lax.axis_size('gz')), out_shape=...  59 us
    unnamed x14, local copies, waits for them, and re-layouts  5.34 us

commit v1 on v0

--- a/solution.py
+++ b/solution.py
@@ -63,10 +63,12 @@
 ]
 DIAGONAL = [(0, 1, 1), (0, 1, -1), (0, -1, 1), (0, -1, -1)]
 
-BLOCKS = 8
-OUTER_BLOCKS = 3
-OUTER_ROWS = 24
-CENTRE_ROWS = 40
+SIZE = 16
+BLOCKS = 4
+OUTER_BLOCKS = 1
+OUTER_ROWS = SIZE * OUTER_BLOCKS
+CENTRE_ROWS = SIZE * (BLOCKS - OUTER_BLOCKS)
+SPAN = 128 // BLOCKS
 N_AXIAL = 0
 N_AXIAL_ROW = 4
 N_ROW = 8
@@ -139,22 +141,74 @@
     return one(high, w_high) + (one(low, w_high) + one(high, w_low))
 
 
+def edge(value, packed, vector):
+    j = EDGES.index(vector)
+    lane = lax.broadcasted_iota(jnp.int32, value.shape, 1)
+    if vector[2] == 1:
+        there = packed if j == 0 else pltpu.roll(packed, 128 - j, 1)
+        return jnp.where(lane == 0, there, value)
+    return jnp.where(lane == 127, pltpu.roll(packed, 127 - j, 1), value)
+
+
+def unpacked(packed, rb):
+    return pltpu.roll(packed, lax.rem(128 - SPAN * rb, 128), 1)
+
+
+def patch(pb, er, pp):
+    def block(rb, carry):
+        row = pl.multiple_of(rb * SIZE + 8, 8)
+        packed = unpacked(er[0], rb)
+        for k, vector in enumerate(DIAGONAL):
+            value = pb[INPLANE.index(vector), pl.ds(row, SIZE), :]
+            pp[k, pl.ds(row, SIZE), :] = edge(value, packed, vector)
+        return carry
+
+    lax.fori_loop(0, BLOCKS, block, 0)
+    before = pltpu.roll(er[1, SIZE - 8 :, :], SPAN, 1)
+    after = er[2, 0:8, :]
+    for k, vector in enumerate(DIAGONAL):
+        packed, row = (before, 0) if vector[1] == 1 else (after, 72)
+        value = pb[INPLANE.index(vector), pl.ds(row, 8), :]
+        pp[k, pl.ds(row, 8), :] = edge(value, packed, vector)
+
+
+def streamed(pb, zr, er, pp, rb):
+    row = pl.multiple_of(rb * SIZE, 8)
+    packed = {0: unpacked(er[0], rb), 1: unpacked(er[3], rb), -1: unpacked(er[4], rb)}
+    f = []
+    for vector in VELOCITIES:
+        rows = pl.ds(row + (8 - vector[1]), SIZE)
+        if vector in DIAGONAL:
+            f.append(pp[DIAGONAL.index(vector), rows, :])
+            continue
+        if vector[0] == 0:
+            value = pb[INPLANE.index(vector), rows, :]
+        else:
+            way = 0 if vector[0] == 1 else 1
+            value = zr[way, AXIAL[way].index(vector), rows, :]
+        if vector[2] != 0:
+            value = edge(value, packed[vector[0]], vector)
+        f.append(value)
+    return f
+
+
 def kernel(
     gz_size,
-    pops,
-    solid,
-    whirl,
-    cells,
-    weights,
-    target,
-    out_pops,
-    out_vel,
-    out_force,
-    pb,
+    pops_in,
+    solid_in,
+    whirl_in,
+    cells_in,
+    weights_in,
+    target_in,
+    pb_last,
+    zr_last,
+    er_last,
+    force_last,
+    pb_early,
     zs,
-    zr,
+    zr_early,
     es,
-    er,
+    er_early,
     pp,
     st,
     mom,
@@ -170,7 +224,32 @@
     recv_sem,
     mk_send,
     mk_recv,
+    pops,
+    solid,
+    whirl,
+    cells,
+    weights,
+    target,
+    load_sem,
 ):
+    loads = [
+        pltpu.make_async_copy(src, dst, load_sem.at[k])
+        for k, (src, dst) in enumerate(
+            [
+                (cells_in, cells),
+                (weights_in, weights),
+                (target_in, target),
+                (whirl_in, whirl),
+                (pops_in, pops),
+                (solid_in, solid),
+            ]
+        )
+    ]
+    for load in loads:
+        load.start()
+    pb = [pb_early.at[s] for s in range(STEPS - 1)] + [pb_last]
+    zr = [zr_early.at[s] for s in range(STEPS - 1)] + [zr_last]
+    er = [er_early.at[s] for s in range(STEPS - 1)] + [er_last]
     gz = lax.axis_index("gz")
     gx = lax.axis_index("gx")
     gy = lax.axis_index("gy")
@@ -183,8 +262,8 @@
     outer = is_centre == 0
     quarter = lax.rem(2 * gx + gy + 2, 4)
     own = 2 * gx + gy
-    outer_start = pl.multiple_of(40 * flip, 8)
-    centre_start = pl.multiple_of(24 * (1 - flip), 8)
+    outer_start = pl.multiple_of(CENTRE_ROWS * flip, 8)
+    centre_start = pl.multiple_of(OUTER_ROWS * (1 - flip), 8)
 
     barrier = pltpu.get_barrier_semaphore()
     neighbours = [
@@ -206,8 +285,8 @@
     for place in neighbours:
         pl.semaphore_signal(barrier, inc=1, device_id=place, device_id_type=MESH)
 
-    lane = lax.broadcasted_iota(jnp.int32, (8, 128), 1)
-    lane_block = lane // 16
+    lanes = lax.broadcasted_iota(jnp.int32, (SIZE, 128), 1)
+    lane_block = lanes // SPAN
 
     def block_of(b):
         return b + flip * (BLOCKS - 1 - 2 * b)
@@ -226,7 +305,7 @@
         start, size = ((outer_start, OUTER_ROWS), (centre_start, CENTRE_ROWS))[part]
         return remote(
             zs.at[s, way, :, pl.ds(start, size), :],
-            zr.at[s, way, :, pl.ds(pl.multiple_of(start + 8, 8), size), :],
+            zr[s].at[way, :, pl.ds(pl.multiple_of(start + 8, 8), size), :],
             s,
             N_AXIAL + 2 * way + part,
             {"gz": (z_next, z_prev)[way], "gx": gx, "gy": gy},
@@ -239,7 +318,7 @@
             copies.append(
                 remote(
                     zs.at[s, way, 3, pl.ds(56, 8), :],
-                    zr.at[s, way, 3, pl.ds(0, 8), :],
+                    zr[s].at[way, 3, pl.ds(0, 8), :],
                     s,
                     N_AXIAL_ROW + 2 * way,
                     {"gz": z, "gx": x_next, "gy": gy},
@@ -248,7 +327,7 @@
             copies.append(
                 remote(
                     zs.at[s, way, 4, pl.ds(0, 8), :],
-                    zr.at[s, way, 4, pl.ds(72, 8), :],
+                    zr[s].at[way, 4, pl.ds(72, 8), :],
                     s,
                     N_AXIAL_ROW + 2 * way + 1,
                     {"gz": z, "gx": x_prev, "gy": gy},
@@ -256,8 +335,8 @@
             )
         copies.append(
             remote(
-                pb.at[s, pl.ds(3, 3), pl.ds(64, 8), :],
-                pb.at[s, pl.ds(3, 3), pl.ds(0, 8), :],
+                pb[s].at[pl.ds(3, 3), pl.ds(64, 8), :],
+                pb[s].at[pl.ds(3, 3), pl.ds(0, 8), :],
                 s,
                 N_ROW,
                 {"gz": gz, "gx": x_next, "gy": gy},
@@ -265,8 +344,8 @@
         )
         copies.append(
             remote(
-                pb.at[s, pl.ds(6, 3), pl.ds(8, 8), :],
-                pb.at[s, pl.ds(6, 3), pl.ds(72, 8), :],
+                pb[s].at[pl.ds(6, 3), pl.ds(8, 8), :],
+                pb[s].at[pl.ds(6, 3), pl.ds(72, 8), :],
                 s,
                 N_ROW + 1,
                 {"gz": gz, "gx": x_prev, "gy": gy},
@@ -280,7 +359,7 @@
             {"gz": z_prev, "gx": gx, "gy": y_other},
         ]
         for k, place in enumerate(places):
-            copies.append(remote(es.at[s], er.at[s, k], s, N_EDGE + k, place))
+            copies.append(remote(es.at[s], er[s].at[k], s, N_EDGE + k, place))
         return copies
 
     def sample_copies(s):
@@ -329,78 +408,34 @@
     def not_self(t):
         return jnp.logical_or(gx != 1 + t // 2, gy != t % 2)
 
-    def edge(value, packed, vector):
-        j = EDGES.index(vector)
-        if vector[2] == 1:
-            there = packed if j == 0 else pltpu.roll(packed, 128 - j, 1)
-            return jnp.where(lane == 0, there, value)
-        return jnp.where(lane == 127, pltpu.roll(packed, 127 - j, 1), value)
-
     def gather(s, rb):
-        row = pl.multiple_of(rb * 8, 8)
         if s == 0:
-            return [pops[m, 0, pl.ds(row, 8), :] for m in range(19)]
-        back = lax.rem(128 - 16 * rb, 128)
-        packed = {
-            0: pltpu.roll(er[s - 1, 0], back, 1),
-            1: pltpu.roll(er[s - 1, 3], back, 1),
-            -1: pltpu.roll(er[s - 1, 4], back, 1),
-        }
-        f = []
-        for vector in VELOCITIES:
-            rows = pl.ds(row + (8 - vector[1]), 8)
-            if vector in DIAGONAL:
-                f.append(pp[DIAGONAL.index(vector), rows, :])
-                continue
-            if vector[0] == 0:
-                value = pb[s - 1, INPLANE.index(vector), rows, :]
-            else:
-                way = 0 if vector[0] == 1 else 1
-                value = zr[s - 1, way, AXIAL[way].index(vector), rows, :]
-            if vector[2] != 0:
-                value = edge(value, packed[vector[0]], vector)
-            f.append(value)
-        return f
-
-    def patch(s):
-        def block(rb, carry):
-            row = pl.multiple_of(rb * 8 + 8, 8)
-            packed = pltpu.roll(er[s - 1, 0], lax.rem(128 - 16 * rb, 128), 1)
-            for k, vector in enumerate(DIAGONAL):
-                value = pb[s - 1, INPLANE.index(vector), pl.ds(row, 8), :]
-                pp[k, pl.ds(row, 8), :] = edge(value, packed, vector)
-            return carry
-
-        lax.fori_loop(0, BLOCKS, block, 0)
-        before = pltpu.roll(er[s - 1, 1], 16, 1)
-        after = er[s - 1, 2]
-        for k, vector in enumerate(DIAGONAL):
-            packed, row = (before, 0) if vector[1] == 1 else (after, 72)
-            value = pb[s - 1, INPLANE.index(vector), pl.ds(row, 8), :]
-            pp[k, pl.ds(row, 8), :] = edge(value, packed, vector)
+            row = pl.multiple_of(rb * SIZE, 8)
+            return [pops[m, 0, pl.ds(row, SIZE), :] for m in range(19)]
+        return streamed(pb[s - 1], zr[s - 1], er[s - 1], pp, rb)
 
     def store_post(s, rb, post):
-        row = pl.multiple_of(rb * 8, 8)
+        row = pl.multiple_of(rb * SIZE, 8)
         for vector in VELOCITIES:
             value = post[INDEX[vector]]
             if vector[2] != 0:
                 value = pltpu.roll(value, 1 if vector[2] == 1 else 127, 1)
             if vector[0] == 0:
-                pb[s, INPLANE.index(vector), pl.ds(pl.multiple_of(row + 8, 8), 8), :] = value
+                pb[s][INPLANE.index(vector), pl.ds(pl.multiple_of(row + 8, 8), SIZE), :] = value
             else:
                 way = 0 if vector[0] == 1 else 1
-                zs[s, way, AXIAL[way].index(vector), pl.ds(row, 8), :] = value
+                zs[s, way, AXIAL[way].index(vector), pl.ds(row, SIZE), :] = value
         packed = post[INDEX[EDGES[0]]]
         packed = pltpu.roll(packed, 1, 1)
         for j, vector in enumerate(EDGES):
             if j == 0:
                 continue
             shift = j + 1 if vector[2] == 1 else j
-            packed = jnp.where(lane == j, pltpu.roll(post[INDEX[vector]], shift, 1), packed)
-        es[s] = jnp.where(lane_block == rb, pltpu.roll(packed, 16 * rb, 1), es[s])
+            packed = jnp.where(lanes == j, pltpu.roll(post[INDEX[vector]], shift, 1), packed)
+        es[s] = jnp.where(lane_block == rb, pltpu.roll(packed, SPAN * rb, 1), es[s])
 
     def fluid_of(rb):
-        return solid[0, pl.ds(pl.multiple_of(rb * 8, 8), 8), :] == 0
+        return solid[0, pl.ds(pl.multiple_of(rb * SIZE, 8), SIZE), :] == 0
 
     def whole_block(s):
         def block(b, carry):
@@ -415,14 +450,14 @@
     def first_half(s):
         def block(b, carry):
             rb = block_of(b)
-            row = pl.multiple_of(rb * 8, 8)
+            row = pl.multiple_of(rb * SIZE, 8)
             f = gather(s, rb)
             density, inverse, u = moments(f)
             if s > 0:
                 for m in range(19):
-                    st[m, pl.ds(row, 8), :] = f[m]
+                    st[m, pl.ds(row, SIZE), :] = f[m]
             for c, value in enumerate([*u, density, inverse]):
-                mom[c, pl.ds(row, 8), :] = value
+                mom[c, pl.ds(row, SIZE), :] = value
             return carry
 
         return block
@@ -430,15 +465,15 @@
     def second_half(s):
         def block(b, carry):
             rb = block_of(b)
-            row = pl.multiple_of(rb * 8, 8)
+            row = pl.multiple_of(rb * SIZE, 8)
             if s == 0:
-                f = [pops[m, 0, pl.ds(row, 8), :] for m in range(19)]
+                f = [pops[m, 0, pl.ds(row, SIZE), :] for m in range(19)]
             else:
-                f = [st[m, pl.ds(row, 8), :] for m in range(19)]
-            density = mom[3, pl.ds(row, 8), :]
-            scale = RELAX_TIME * mom[4, pl.ds(row, 8), :]
+                f = [st[m, pl.ds(row, SIZE), :] for m in range(19)]
+            density = mom[3, pl.ds(row, SIZE), :]
+            scale = RELAX_TIME * mom[4, pl.ds(row, SIZE), :]
             near = pl.multiple_of(row - centre_start, 8)
-            u = [mom[c, pl.ds(row, 8), :] + scale * fb[c, pl.ds(near, 8), :] for c in range(3)]
+            u = [mom[c, pl.ds(row, SIZE), :] + scale * fb[c, pl.ds(near, SIZE), :] for c in range(3)]
             store_post(s, rb, collide(f, density, u, fluid_of(rb)))
             return carry
 
@@ -453,8 +488,8 @@
                 result = jnp.where(distance == float(a), mk[row + a : row + a + 1, :], result)
             return result
 
-        base_x = mk[0:1, :] + (127 + whirl[s, 0]).astype(jnp.float32)
-        base_y = mk[1:2, :] + (127 + whirl[s, 1]).astype(jnp.float32)
+        base_x = mk[0:1, :] + (127 + whirl[0, s]).astype(jnp.float32)
+        base_y = mk[1:2, :] + (127 + whirl[1, s]).astype(jnp.float32)
         wx[...] = matrix(CENTRE_ROWS, 64 * gx + centre_start, base_x, 2)
         high, low = split(matrix(128, 128 * gy, base_y, 6))
         wy_high[...] = high
@@ -480,6 +515,8 @@
         body = product(weighted, wy_high[...], wy_low[...], ((1,), (1,)))
         fb[...] = body.reshape(3, CENTRE_ROWS, 128)
 
+    for load in loads[:4]:
+        load.wait()
     mk_own[...] = jnp.zeros((16, 128), jnp.float32)
     mk_own[0:2, 0:32] = cells[:, 0, :].astype(jnp.float32)
     mk_own[2:6, 0:32] = weights[0, :, 0, :]
@@ -495,12 +532,15 @@
         def _(t=t):
             marker_copy(t).start()
 
+    for load in loads[4:]:
+        load.wait()
+
     for s in range(STEPS):
         last = s == STEPS - 1
         if s > 0:
             for copy in [axial(s - 1, way, part) for way in range(2) for part in range(2)] + small(s - 1):
                 copy.wait_recv()
-            patch(s)
+            patch(pb[s - 1], er[s - 1], pp)
 
         @pl.when(centre)
         def _(s=s):
@@ -530,10 +570,10 @@
             force(s)
             lax.fori_loop(OUTER_BLOCKS, BLOCKS, second_half(s), 0)
 
+        for copy in small(s)[::-1]:
+            copy.start()
         for way in range(2):
             axial(s, way, 1).start()
-        for copy in small(s):
-            copy.start()
 
         if not last:
 
@@ -543,20 +583,6 @@
 
     for copy in [axial(STEPS - 1, way, part) for way in range(2) for part in range(2)] + small(STEPS - 1):
         copy.wait_recv()
-    patch(STEPS)
-
-    def final_block(rb, carry):
-        rows = pl.ds(pl.multiple_of(rb * 8, 8), 8)
-        f = gather(STEPS, rb)
-        for m in range(19):
-            out_pops[m, 0, rows, :] = f[m]
-        _, _, u = moments(f)
-        fluid = fluid_of(rb)
-        for c in range(3):
-            out_vel[c, 0, rows, :] = jnp.where(fluid, u[c] * (1.0 / SPEED_SCALE), 0.0)
-        return carry
-
-    lax.fori_loop(0, BLOCKS, final_block, 0)
 
     @pl.when(outer)
     def _():
@@ -566,7 +592,7 @@
     total = sampled(STEPS - 1)
     half = jnp.where(own // 4 == 0, total[:, 0:128], total[:, 128:256])
     half = pltpu.roll(half, lax.rem(128 - 32 * lax.rem(own, 4), 128), 1)
-    out_force[:, 0, :] = (target[:, 0, :] - half[0:3, 0:32]) * (1.0 / SPEED_SCALE)
+    force_last[:, 0, :] = (target[:, 0, :] - half[0:3, 0:32]) * (1.0 / SPEED_SCALE)
 
     for t in range(4):
 
@@ -585,24 +611,47 @@
                 copy.wait_send()
 
 
+def finish(pb, zr, er, force, solid, res_pops, res_vel, res_force, pp, out_pops, out_vel, sem):
+    patch(pb, er, pp)
+    copies = []
+    for rb in range(BLOCKS):
+        rows = pl.ds(rb * SIZE, SIZE)
+        f = streamed(pb, zr, er, pp, rb)
+        for m in range(19):
+            out_pops[m, 0, rows, :] = f[m]
+        _, _, u = moments(f)
+        fluid = solid[0, rows, :] == 0
+        for c in range(3):
+            out_vel[c, 0, rows, :] = jnp.where(fluid, u[c] * (1.0 / SPEED_SCALE), 0.0)
+        for k, (src, dst) in enumerate([(out_pops, res_pops), (out_vel, res_vel)]):
+            copy = pltpu.make_async_copy(
+                src.at[:, :, rows, :], dst.at[:, :, rows, :], sem.at[2 * rb + k]
+            )
+            copy.start()
+            copies.append(copy)
+    copy = pltpu.make_async_copy(force, res_force, sem.at[2 * BLOCKS])
+    copy.start()
+    copies.append(copy)
+    for copy in copies:
+        copy.wait()
+
+
 def body(populations, solid_mask, whirl_offsets, marker_cells, marker_weights, pipe_velocity):
     f32 = jnp.float32
     vmem = pl.BlockSpec(memory_space=pltpu.VMEM)
-    return pl.pallas_call(
+    hbm = pl.BlockSpec(memory_space=pltpu.HBM)
+    pb, zr, er = (9, 80, 128), (2, 5, 80, 128), (5, SIZE, 128)
+    arrived = pl.pallas_call(
         functools.partial(kernel, lax.axis_size("gz")),
-        out_shape=(
-            jax.ShapeDtypeStruct(populations.shape, f32),
-            jax.ShapeDtypeStruct((3,) + solid_mask.shape, f32),
-            jax.ShapeDtypeStruct(pipe_velocity.shape, f32),
-        ),
-        in_specs=[vmem, vmem, pl.BlockSpec(memory_space=pltpu.SMEM), vmem, vmem, vmem],
-        out_specs=(vmem, vmem, vmem),
+        out_shape=[pltpu.VMEM(shape, f32) for shape in (pb, zr, er, pipe_velocity.shape)],
+        in_specs=[hbm] * 6,
+        out_specs=[vmem] * 4,
         scratch_shapes=[
-            pltpu.VMEM((STEPS, 9, 80, 128), f32),
+            pltpu.VMEM((STEPS - 1,) + pb, f32),
             pltpu.VMEM((STEPS, 2, 5, 64, 128), f32),
-            pltpu.VMEM((STEPS, 2, 5, 80, 128), f32),
-            pltpu.VMEM((STEPS, 8, 128), f32),
-            pltpu.VMEM((STEPS, 5, 8, 128), f32),
+            pltpu.VMEM((STEPS - 1,) + zr, f32),
+            pltpu.VMEM((STEPS, SIZE, 128), f32),
+            pltpu.VMEM((STEPS - 1,) + er, f32),
             pltpu.VMEM((4, 80, 128), f32),
             pltpu.VMEM((19, 64, 128), f32),
             pltpu.VMEM((5, 64, 128), f32),
@@ -618,12 +667,31 @@
             pltpu.SemaphoreType.DMA((STEPS, N_MESSAGES)),
             pltpu.SemaphoreType.DMA((4,)),
             pltpu.SemaphoreType.DMA((8,)),
+            pltpu.VMEM(populations.shape, f32),
+            pltpu.VMEM(solid_mask.shape, jnp.int32),
+            pltpu.SMEM(whirl_offsets.shape[::-1], jnp.int32),
+            pltpu.VMEM(marker_cells.shape, jnp.int32),
+            pltpu.VMEM(marker_weights.shape, f32),
+            pltpu.VMEM(pipe_velocity.shape, f32),
+            pltpu.SemaphoreType.DMA((6,)),
         ],
         compiler_params=pltpu.CompilerParams(
-            collective_id=0, has_side_effects=True, vmem_limit_bytes=24 * 1024 * 1024
+            collective_id=0, has_side_effects=True, vmem_limit_bytes=60 * 1024 * 1024
         ),
         cost_estimate=pl.CostEstimate(flops=40_000_000, bytes_accessed=2_000_000, transcendentals=0),
-    )(populations, solid_mask, whirl_offsets, marker_cells, marker_weights, pipe_velocity)
+    )(populations, solid_mask, whirl_offsets.T, marker_cells, marker_weights, pipe_velocity)
+    shapes = (populations.shape, (3,) + solid_mask.shape, pipe_velocity.shape)
+    return pl.pallas_call(
+        finish,
+        out_shape=[jax.ShapeDtypeStruct(shape, f32) for shape in shapes],
+        in_specs=[vmem] * 5,
+        out_specs=[hbm] * 3,
+        scratch_shapes=[pltpu.VMEM((4, 80, 128), f32)]
+        + [pltpu.VMEM(shape, f32) for shape in shapes[:2]]
+        + [pltpu.SemaphoreType.DMA((2 * BLOCKS + 1,))],
+        compiler_params=pltpu.CompilerParams(vmem_limit_bytes=24 * 1024 * 1024),
+        cost_estimate=pl.CostEstimate(flops=2_000_000, bytes_accessed=2_000_000, transcendentals=0),
+    )(*arrived, solid_mask)
 
 
 def solution(mesh):

time: 65.3 us -> 53.8 us (0.82)
  Pallas kernels: 59 us -> 53 us
  local copies, waits for them, and re-layouts: 5.34 us -> 0.01 us
    pallas_call x1, Pallas kernels: 59 us -> 51.4 us  [body(): pl.pallas_call(functools.partial(kernel, lax.axis_size('gz')), out_shape=...]
    unnamed x14 -> x2, local copies, waits for them, and re-layouts: 5.34 us -> 0.01 us
    pallas_call x0 -> x1, Pallas kernels: none -> 1.58 us  [body(): pl.pallas_call(finish, out_shape=[jax.ShapeDtypeStruct(shape, f32) for sh...]
where the time goes in v1:
time: 53.8 us; the launch traced here: 53.7 us
  Pallas kernels  53 us (99%)
  between operations  0.66 us (1%)
    pallas_call x1, Pallas kernels, body(): pl.pallas_call(functools.partial(kernel, lax.axis_size('gz')), out_shape=...  51.4 us
    pallas_call x1, Pallas kernels, body(): pl.pallas_call(finish, out_shape=[jax.ShapeDtypeStruct(shape, f32) for sh...  1.58 us

profile of v1, /device:TPU:1, one launch (start us, length us, event | category | flops | bytes accessed | tf_op | source)
XLA Modules:
  0.0 53.7 jit_solution(11991099127788801073)
XLA Ops:
  0.6 0.0 copy-start
  0.6 51.4 %shard_map.85 = (f32[9,80,128]{2,1,0:T(8,128)S(1)}, f32[2,5,80,128]{3,2,1,0:T(8,128)S(1)}, f32[5,16,128]{2,1,0:T(8,128)S(1)}, f32[3,1,32]{2,1,0:T(1,128)S(1)}) custom-call(f32[19,1,64,128]{3,2,1,0:T(8,128)} %pops_in.1, s32[1,64,128]{2,1,0:T(8,128)} %solid.1, s32[2,3]{1,0:T(2,128)} %bitcast.1, s32[2,1,32]{2,1,0:T(1,128)} %cells_in.1, ...), custom_call_target="tpu_custom_call" | custom-call | flops 40000000 | bytes 2000000 | tf_op jit(solution)/shard_map/pallas_call | solution.py:644
  52.1 0.0 copy-done
  52.1 1.6 %shard_map.86 = (f32[19,1,64,128]{3,2,1,0:T(8,128)}, f32[3,1,64,128]{3,2,1,0:T(8,128)}, f32[3,1,32]{2,1,0:T(1,128)}) custom-call(f32[9,80,128]{2,1,0:T(8,128)S(1)} %get-tuple-element.7.pb, f32[2,5,80,128]{3,2,1,0:T(8,128)S(1)} %get-tuple-element.8.zr, f32[5,16,128]{2,1,0:T(8,128)S(1)} %get-tuple-element.9.er, f32[3,1,32]{2,1,0:T(1,128)S(1)} %get-tuple-element.10.force, ...), custom_call_target="tpu_custom_call" | custom-call | flops 2000000 | bytes 2000000 | tf_op jit(solution)/shard_map/pallas_call | solution.py:684
Async XLA Ops:
  0.6 51.4 %copy-start = (s32[1,64,128]{2,1,0:T(8,128)S(1)}, s32[1,64,128]{2,1,0:T(8,128)}, u32[]{:S(2)}) copy-start(s32[1,64,128]{2,1,0:T(8,128)} %solid.1) | copy-start | bytes 98308

commit v2 on v1

--- a/solution.py
+++ b/solution.py
@@ -163,7 +163,7 @@
             pp[k, pl.ds(row, SIZE), :] = edge(value, packed, vector)
         return carry
 
-    lax.fori_loop(0, BLOCKS, block, 0)
+    lax.fori_loop(0, BLOCKS, block, 0, unroll=True)
     before = pltpu.roll(er[1, SIZE - 8 :, :], SPAN, 1)
     after = er[2, 0:8, :]
     for k, vector in enumerate(DIAGONAL):
@@ -544,7 +544,7 @@
 
         @pl.when(centre)
         def _(s=s):
-            lax.fori_loop(OUTER_BLOCKS, BLOCKS, first_half(s), 0)
+            lax.fori_loop(OUTER_BLOCKS, BLOCKS, first_half(s), 0, unroll=True)
             if s == 0:
                 for d in range(1, 8):
                     marker_wait(lax.rem(own + d, 8))
@@ -555,20 +555,20 @@
             for copy in sample_copies(s):
                 copy.start()
 
-        lax.fori_loop(0, OUTER_BLOCKS, whole_block(s), 0)
+        lax.fori_loop(0, OUTER_BLOCKS, whole_block(s), 0, unroll=True)
         for way in range(2):
             axial(s, way, 0).start()
 
         @pl.when(outer)
         def _(s=s):
-            lax.fori_loop(OUTER_BLOCKS, BLOCKS, whole_block(s), 0)
+            lax.fori_loop(OUTER_BLOCKS, BLOCKS, whole_block(s), 0, unroll=True)
 
         @pl.when(centre)
         def _(s=s):
             for d in range(1, 4):
                 sample_wait(s, lax.rem(quarter + d, 4))
             force(s)
-            lax.fori_loop(OUTER_BLOCKS, BLOCKS, second_half(s), 0)
+            lax.fori_loop(OUTER_BLOCKS, BLOCKS, second_half(s), 0, unroll=True)
 
         for copy in small(s)[::-1]:
             copy.start()

time: 53.8 us -> 50.8 us (0.944)
  Pallas kernels: 53 us -> 50 us
    pallas_call x1, Pallas kernels: 51.4 us -> 48.9 us  [body(): pl.pallas_call(functools.partial(kernel, lax.axis_size('gz')), out_shape=...]
where the time goes in v2:
time: 50.8 us; the launch traced here: 50.7 us
  Pallas kernels  50 us (98%)
  between operations  0.66 us (1%)
    pallas_call x1, Pallas kernels, body(): pl.pallas_call(functools.partial(kernel, lax.axis_size('gz')), out_shape=...  48.9 us
    pallas_call x1, Pallas kernels, body(): pl.pallas_call(finish, out_shape=[jax.ShapeDtypeStruct(shape, f32) for sh...  1.1 us

profile of v2, /device:TPU:1, one launch (start us, length us, event | category | flops | bytes accessed | tf_op | source)
XLA Modules:
  0.0 50.7 jit_solution(15061099096714595306)
XLA Ops:
  0.6 0.0 copy-start
  0.6 48.9 %shard_map.85 = (f32[9,80,128]{2,1,0:T(8,128)S(1)}, f32[2,5,80,128]{3,2,1,0:T(8,128)S(1)}, f32[5,16,128]{2,1,0:T(8,128)S(1)}, f32[3,1,32]{2,1,0:T(1,128)S(1)}) custom-call(f32[19,1,64,128]{3,2,1,0:T(8,128)} %pops_in.1, s32[1,64,128]{2,1,0:T(8,128)} %solid.1, s32[2,3]{1,0:T(2,128)} %bitcast.1, s32[2,1,32]{2,1,0:T(1,128)} %cells_in.1, ...), custom_call_target="tpu_custom_call" | custom-call | flops 40000000 | bytes 2000000 | tf_op jit(solution)/shard_map/pallas_call | solution.py:644
  49.5 0.0 copy-done
  49.6 1.1 %shard_map.86 = (f32[19,1,64,128]{3,2,1,0:T(8,128)}, f32[3,1,64,128]{3,2,1,0:T(8,128)}, f32[3,1,32]{2,1,0:T(1,128)}) custom-call(f32[9,80,128]{2,1,0:T(8,128)S(1)} %get-tuple-element.7.pb, f32[2,5,80,128]{3,2,1,0:T(8,128)S(1)} %get-tuple-element.8.zr, f32[5,16,128]{2,1,0:T(8,128)S(1)} %get-tuple-element.9.er, f32[3,1,32]{2,1,0:T(1,128)S(1)} %get-tuple-element.10.force, ...), custom_call_target="tpu_custom_call" | custom-call | flops 2000000 | bytes 2000000 | tf_op jit(solution)/shard_map/pallas_call | solution.py:684
Async XLA Ops:
  0.6 48.9 %copy-start = (s32[1,64,128]{2,1,0:T(8,128)S(1)}, s32[1,64,128]{2,1,0:T(8,128)}, u32[]{:S(2)}) copy-start(s32[1,64,128]{2,1,0:T(8,128)} %solid.1) | copy-start | bytes 98308

commit v3 on v2

--- a/solution.py
+++ b/solution.py
@@ -74,6 +74,7 @@
 N_ROW = 8
 N_EDGE = 10
 N_SAMPLE = 15
+N_STRIP = 22
 N_MESSAGES = 24
 
 
@@ -230,7 +231,12 @@
     cells,
     weights,
     target,
+    strip_out,
+    strip_in,
+    rows_in,
+    full,
     load_sem,
+    vouch_sem,
 ):
     loads = [
         pltpu.make_async_copy(src, dst, load_sem.at[k])
@@ -276,12 +282,7 @@
         {"gz": gz, "gx": x_far, "gy": y_other},
     ]
     for z in (z_next, z_prev):
-        neighbours += [
-            {"gz": z, "gx": gx, "gy": gy},
-            {"gz": z, "gx": x_next, "gy": gy},
-            {"gz": z, "gx": x_prev, "gy": gy},
-            {"gz": z, "gx": gx, "gy": y_other},
-        ]
+        neighbours.append({"gz": z, "gx": gx, "gy": gy})
     for place in neighbours:
         pl.semaphore_signal(barrier, inc=1, device_id=place, device_id_type=MESH)
 
@@ -382,6 +383,19 @@
     def sample_wait(s, q):
         remote(sp.at[s, q], sp.at[s, q], s, N_SAMPLE, neighbours[0], N_SAMPLE + q).wait_recv()
 
+    def strip_copies():
+        edge_rows = pl.ds(pl.multiple_of(56 - 56 * flip, 8), 8)
+        return [
+            remote(
+                mom.at[pl.ds(0, 3), edge_rows, :],
+                rows_in,
+                0,
+                N_STRIP,
+                {"gz": gz, "gx": 3 - gx, "gy": gy},
+            ),
+            remote(strip_out, strip_in, 0, N_STRIP + 1, {"gz": gz, "gx": gx, "gy": y_other}),
+        ]
+
     def centre_place(t):
         return {"gz": gz, "gx": 1 + t // 2, "gy": t % 2}
 
@@ -479,19 +493,19 @@
 
         return block
 
+    def matrix(s, size, first, dim):
+        base = mk[dim : dim + 1, :] + (127 + whirl[dim, s]).astype(jnp.float32)
+        place = lax.broadcasted_iota(jnp.int32, (size, 256), 0) + first
+        distance = place.astype(jnp.float32) - base
+        result = jnp.zeros((size, 256), jnp.float32)
+        for a in range(4):
+            row = 2 + 4 * dim + a
+            result = jnp.where(distance == float(a), mk[row : row + 1, :], result)
+        return result
+
     def marker_matrices(s):
-        def matrix(size, first, base, row):
-            place = lax.broadcasted_iota(jnp.int32, (size, 256), 0) + first
-            distance = place.astype(jnp.float32) - base
-            result = jnp.zeros((size, 256), jnp.float32)
-            for a in range(4):
-                result = jnp.where(distance == float(a), mk[row + a : row + a + 1, :], result)
-            return result
-
-        base_x = mk[0:1, :] + (127 + whirl[0, s]).astype(jnp.float32)
-        base_y = mk[1:2, :] + (127 + whirl[1, s]).astype(jnp.float32)
-        wx[...] = matrix(CENTRE_ROWS, 64 * gx + centre_start, base_x, 2)
-        high, low = split(matrix(128, 128 * gy, base_y, 6))
+        wx[...] = matrix(s, CENTRE_ROWS, 64 * gx + centre_start, 0)
+        high, low = split(matrix(s, 128, 128 * gy, 1))
         wy_high[...] = high
         wy_low[...] = low
 
@@ -505,11 +519,48 @@
         ]
         sp[s, quarter] = jnp.concatenate(rows + [jnp.zeros((5, 256), jnp.float32)], axis=0)
 
+    def pack_strips():
+        packed = jnp.zeros((SIZE, 128), jnp.float32)
+        for c in range(3):
+            for b in range(CENTRE_ROWS // SIZE):
+                value = mom[c, pl.ds(pl.multiple_of(centre_start + SIZE * b, 8), SIZE), :]
+                first = 4 * (3 * c + b)
+                value = pltpu.roll(value, first + 4 * (1 - gy), 1)
+                packed = jnp.where((lanes >= first) & (lanes < first + 4), value, packed)
+        strip_out[...] = packed
+
+    def sample_full():
+        u = mom[0:3, pl.ds(centre_start, CENTRE_ROWS), :].reshape(3 * CENTRE_ROWS, 128)
+        beside = rows_in[...].reshape(24, 128)
+        along = product(
+            jnp.concatenate([u, beside], axis=0), wy_high[...], wy_low[...], ((1,), (0,))
+        )
+        spread = wx[...]
+        spread_beside = matrix(0, 8, 64 * gx + 64 - 72 * flip, 0)
+        wanted = jnp.where(gy == 0, lanes, 127 - lanes) < 4
+        packed = strip_in[...]
+        pieces = []
+        for c in range(3):
+            for b in range(CENTRE_ROWS // SIZE):
+                shift = lax.rem(256 - 4 * (3 * c + b) - 4 * gy, 128)
+                pieces.append(jnp.where(wanted, pltpu.roll(packed, shift, 1), 0.0))
+        across = product(
+            jnp.concatenate(pieces, axis=0), *split(matrix(0, 128, 128 * (1 - gy), 1)), ((1,), (0,))
+        )
+        rows = []
+        for c in range(3):
+            part = slice(c * CENTRE_ROWS, (c + 1) * CENTRE_ROWS)
+            first = 3 * CENTRE_ROWS + 8 * c
+            total = jnp.sum((along[part] + across[part]) * spread, axis=0, keepdims=True)
+            total += jnp.sum(along[first : first + 8] * spread_beside, axis=0, keepdims=True)
+            rows.append(total)
+        full[...] = jnp.concatenate(rows, axis=0)
+
     def sampled(s):
         return (sp[s, 0] + sp[s, 1]) + (sp[s, 2] + sp[s, 3])
 
     def force(s):
-        push = mk[10:13, :] - sampled(s)[0:3, :]
+        push = mk[10:13, :] - (full[...] if s == 0 else sampled(s)[0:3, :])
         spread = wx[...]
         weighted = jnp.concatenate([spread * push[c : c + 1, :] for c in range(3)], axis=0)
         body = product(weighted, wy_high[...], wy_low[...], ((1,), (1,)))
@@ -525,6 +576,9 @@
     mk_all[own] = pltpu.roll(mk_own[...], 32 * lax.rem(own, 4), 1)
 
     pl.semaphore_wait(barrier, len(neighbours))
+    vouched = [neighbours[0], neighbours[1], neighbours[3]]
+    for place in vouched:
+        pl.semaphore_signal(vouch_sem, inc=1, device_id=place, device_id_type=MESH)
 
     for t in range(4):
 
@@ -544,32 +598,46 @@
 
         @pl.when(centre)
         def _(s=s):
+            if s == 1:
+                for copy in strip_copies():
+                    copy.wait_send()
             lax.fori_loop(OUTER_BLOCKS, BLOCKS, first_half(s), 0, unroll=True)
+            if s == 0:
+                pack_strips()
+                for copy in strip_copies():
+                    copy.start()
+            else:
+                sample(s)
+                for copy in sample_copies(s):
+                    copy.start()
+
+        lax.fori_loop(0, OUTER_BLOCKS, whole_block(s), 0, unroll=True)
+        for way in range(2):
+            axial(s, way, 0).start()
+
+        @pl.when(outer)
+        def _(s=s):
+            lax.fori_loop(OUTER_BLOCKS, BLOCKS, whole_block(s), 0, unroll=True)
+
+        @pl.when(centre)
+        def _(s=s):
             if s == 0:
                 for d in range(1, 8):
                     marker_wait(lax.rem(own + d, 8))
                 mk[:, 0:128] = (mk_all[0] + mk_all[1]) + (mk_all[2] + mk_all[3])
                 mk[:, 128:256] = (mk_all[4] + mk_all[5]) + (mk_all[6] + mk_all[7])
                 marker_matrices(s)
-            sample(s)
-            for copy in sample_copies(s):
-                copy.start()
-
-        lax.fori_loop(0, OUTER_BLOCKS, whole_block(s), 0, unroll=True)
-        for way in range(2):
-            axial(s, way, 0).start()
-
-        @pl.when(outer)
-        def _(s=s):
-            lax.fori_loop(OUTER_BLOCKS, BLOCKS, whole_block(s), 0, unroll=True)
-
-        @pl.when(centre)
-        def _(s=s):
-            for d in range(1, 4):
-                sample_wait(s, lax.rem(quarter + d, 4))
+                for copy in strip_copies():
+                    copy.wait_recv()
+                sample_full()
+            else:
+                for d in range(1, 4):
+                    sample_wait(s, lax.rem(quarter + d, 4))
             force(s)
             lax.fori_loop(OUTER_BLOCKS, BLOCKS, second_half(s), 0, unroll=True)
 
+        if s == 0:
+            pl.semaphore_wait(vouch_sem, len(vouched))
         for copy in small(s)[::-1]:
             copy.start()
         for way in range(2):
@@ -606,7 +674,7 @@
 
     @pl.when(centre)
     def _():
-        for s in range(STEPS):
+        for s in range(1, STEPS):
             for copy in sample_copies(s):
                 copy.wait_send()
 
@@ -673,7 +741,12 @@
             pltpu.VMEM(marker_cells.shape, jnp.int32),
             pltpu.VMEM(marker_weights.shape, f32),
             pltpu.VMEM(pipe_velocity.shape, f32),
+            pltpu.VMEM((SIZE, 128), f32),
+            pltpu.VMEM((SIZE, 128), f32),
+            pltpu.VMEM((3, 8, 128), f32),
+            pltpu.VMEM((3, 256), f32),
             pltpu.SemaphoreType.DMA((6,)),
+            pltpu.SemaphoreType.REGULAR,
         ],
         compiler_params=pltpu.CompilerParams(
             collective_id=0, has_side_effects=True, vmem_limit_bytes=60 * 1024 * 1024

time: 50.8 us -> 47.2 us (0.929)
  Pallas kernels: 50 us -> 46.3 us
    pallas_call x1, Pallas kernels: 48.9 us -> 45.2 us  [body(): pl.pallas_call(functools.partial(kernel, lax.axis_size('gz')), out_shape=...]
where the time goes in v3:
time: 47.2 us; the launch traced here: 47 us
  Pallas kernels  46.3 us (98%)
  between operations  0.66 us (1%)
    pallas_call x1, Pallas kernels, body(): pl.pallas_call(functools.partial(kernel, lax.axis_size('gz')), out_shape=...  45.2 us
    pallas_call x1, Pallas kernels, body(): pl.pallas_call(finish, out_shape=[jax.ShapeDtypeStruct(shape, f32) for sh...  1.1 us

profile of v3, /device:TPU:1, one launch (start us, length us, event | category | flops | bytes accessed | tf_op | source)
XLA Modules:
  0.0 47.0 jit_solution(15281098876369279078)
XLA Ops:
  0.6 0.0 copy-start
  0.6 45.2 %shard_map.85 = (f32[9,80,128]{2,1,0:T(8,128)S(1)}, f32[2,5,80,128]{3,2,1,0:T(8,128)S(1)}, f32[5,16,128]{2,1,0:T(8,128)S(1)}, f32[3,1,32]{2,1,0:T(1,128)S(1)}) custom-call(f32[19,1,64,128]{3,2,1,0:T(8,128)} %pops_in.1, s32[1,64,128]{2,1,0:T(8,128)} %solid.1, s32[2,3]{1,0:T(2,128)} %bitcast.1, s32[2,1,32]{2,1,0:T(1,128)} %cells_in.1, ...), custom_call_target="tpu_custom_call" | custom-call | flops 40000000 | bytes 2000000 | tf_op jit(solution)/shard_map/pallas_call | solution.py:712
  45.9 0.0 copy-done
  45.9 1.1 %shard_map.86 = (f32[19,1,64,128]{3,2,1,0:T(8,128)}, f32[3,1,64,128]{3,2,1,0:T(8,128)}, f32[3,1,32]{2,1,0:T(1,128)}) custom-call(f32[9,80,128]{2,1,0:T(8,128)S(1)} %get-tuple-element.7.pb, f32[2,5,80,128]{3,2,1,0:T(8,128)S(1)} %get-tuple-element.8.zr, f32[5,16,128]{2,1,0:T(8,128)S(1)} %get-tuple-element.9.er, f32[3,1,32]{2,1,0:T(1,128)S(1)} %get-tuple-element.10.force, ...), custom_call_target="tpu_custom_call" | custom-call | flops 2000000 | bytes 2000000 | tf_op jit(solution)/shard_map/pallas_call | solution.py:757
Async XLA Ops:
  0.6 45.2 %copy-start = (s32[1,64,128]{2,1,0:T(8,128)S(1)}, s32[1,64,128]{2,1,0:T(8,128)}, u32[]{:S(2)}) copy-start(s32[1,64,128]{2,1,0:T(8,128)} %solid.1) | copy-start | bytes 98308

commit v4 on v3

--- a/solution.py
+++ b/solution.py
@@ -63,11 +63,12 @@
 ]
 DIAGONAL = [(0, 1, 1), (0, 1, -1), (0, -1, 1), (0, -1, -1)]
 
-SIZE = 16
-BLOCKS = 4
-OUTER_BLOCKS = 1
+SIZE = 8
+BLOCKS = 8
+OUTER_BLOCKS = 3
 OUTER_ROWS = SIZE * OUTER_BLOCKS
-CENTRE_ROWS = SIZE * (BLOCKS - OUTER_BLOCKS)
+CENTRE_BLOCKS = BLOCKS - OUTER_BLOCKS
+CENTRE_ROWS = SIZE * CENTRE_BLOCKS
 SPAN = 128 // BLOCKS
 N_AXIAL = 0
 N_AXIAL_ROW = 4
@@ -522,9 +523,9 @@
     def pack_strips():
         packed = jnp.zeros((SIZE, 128), jnp.float32)
         for c in range(3):
-            for b in range(CENTRE_ROWS // SIZE):
+            for b in range(CENTRE_BLOCKS):
                 value = mom[c, pl.ds(pl.multiple_of(centre_start + SIZE * b, 8), SIZE), :]
-                first = 4 * (3 * c + b)
+                first = 4 * (CENTRE_BLOCKS * c + b)
                 value = pltpu.roll(value, first + 4 * (1 - gy), 1)
                 packed = jnp.where((lanes >= first) & (lanes < first + 4), value, packed)
         strip_out[...] = packed
@@ -541,8 +542,8 @@
         packed = strip_in[...]
         pieces = []
         for c in range(3):
-            for b in range(CENTRE_ROWS // SIZE):
-                shift = lax.rem(256 - 4 * (3 * c + b) - 4 * gy, 128)
+            for b in range(CENTRE_BLOCKS):
+                shift = lax.rem(256 - 4 * (CENTRE_BLOCKS * c + b) - 4 * gy, 128)
                 pieces.append(jnp.where(wanted, pltpu.roll(packed, shift, 1), 0.0))
         across = product(
             jnp.concatenate(pieces, axis=0), *split(matrix(0, 128, 128 * (1 - gy), 1)), ((1,), (0,))
@@ -649,9 +650,6 @@
             def _(s=s):
                 marker_matrices(s + 1)
 
-    for copy in [axial(STEPS - 1, way, part) for way in range(2) for part in range(2)] + small(STEPS - 1):
-        copy.wait_recv()
-
     @pl.when(outer)
     def _():
         for q in range(4):
@@ -667,16 +665,21 @@
         @pl.when(not_self(t))
         def _(t=t):
             marker_copy(t).wait_send()
-
-    for s in range(STEPS):
-        for copy in [axial(s, way, part) for way in range(2) for part in range(2)] + small(s):
-            copy.wait_send()
 
     @pl.when(centre)
     def _():
         for s in range(1, STEPS):
             for copy in sample_copies(s):
                 copy.wait_send()
+
+    for s in range(STEPS):
+        for copy in small(s) + [axial(s, way, part) for part in range(2) for way in range(2)]:
+            copy.wait_send()
+
+    for copy in small(STEPS - 1)[::-1] + [
+        axial(STEPS - 1, way, part) for part in range(2) for way in range(2)
+    ]:
+        copy.wait_recv()
 
 
 def finish(pb, zr, er, force, solid, res_pops, res_vel, res_force, pp, out_pops, out_vel, sem):

time: 47.2 us -> 46.3 us (0.981)
  Pallas kernels: 46.3 us -> 45.5 us
    pallas_call x1, Pallas kernels: 45.2 us -> 44.3 us  [body(): pl.pallas_call(functools.partial(kernel, lax.axis_size('gz')), out_shape=...]
where the time goes in v4:
time: 46.3 us; the launch traced here: 46.1 us
  Pallas kernels  45.5 us (98%)
  between operations  0.66 us (1%)
    pallas_call x1, Pallas kernels, body(): pl.pallas_call(functools.partial(kernel, lax.axis_size('gz')), out_shape=...  44.3 us
    pallas_call x1, Pallas kernels, body(): pl.pallas_call(finish, out_shape=[jax.ShapeDtypeStruct(shape, f32) for sh...  1.15 us

profile of v4, /device:TPU:1, one launch (start us, length us, event | category | flops | bytes accessed | tf_op | source)
XLA Modules:
  0.0 46.1 jit_solution(4885786640274148088)
XLA Ops:
  0.6 0.0 copy-start
  0.6 44.3 %shard_map.85 = (f32[9,80,128]{2,1,0:T(8,128)S(1)}, f32[2,5,80,128]{3,2,1,0:T(8,128)S(1)}, f32[5,8,128]{2,1,0:T(8,128)S(1)}, f32[3,1,32]{2,1,0:T(1,128)S(1)}) custom-call(f32[19,1,64,128]{3,2,1,0:T(8,128)} %pops_in.1, s32[1,64,128]{2,1,0:T(8,128)} %solid.1, s32[2,3]{1,0:T(2,128)} %bitcast.1, s32[2,1,32]{2,1,0:T(1,128)} %cells_in.1, ...), custom_call_target="tpu_custom_call" | custom-call | flops 40000000 | bytes 2000000 | tf_op jit(solution)/shard_map/pallas_call | solution.py:715
  45.0 0.0 copy-done
  45.0 1.2 %shard_map.86 = (f32[19,1,64,128]{3,2,1,0:T(8,128)}, f32[3,1,64,128]{3,2,1,0:T(8,128)}, f32[3,1,32]{2,1,0:T(1,128)}) custom-call(f32[9,80,128]{2,1,0:T(8,128)S(1)} %get-tuple-element.7.pb, f32[2,5,80,128]{3,2,1,0:T(8,128)S(1)} %get-tuple-element.8.zr, f32[5,8,128]{2,1,0:T(8,128)S(1)} %get-tuple-element.9.er, f32[3,1,32]{2,1,0:T(1,128)S(1)} %get-tuple-element.10.force, ...), custom_call_target="tpu_custom_call" | custom-call | flops 2000000 | bytes 2000000 | tf_op jit(solution)/shard_map/pallas_call | solution.py:760
Async XLA Ops:
  0.6 44.3 %copy-start = (s32[1,64,128]{2,1,0:T(8,128)S(1)}, s32[1,64,128]{2,1,0:T(8,128)}, u32[]{:S(2)}) copy-start(s32[1,64,128]{2,1,0:T(8,128)} %solid.1) | copy-start | bytes 98308

commit v5 on v4

--- a/solution.py
+++ b/solution.py
@@ -269,6 +269,8 @@
     outer = is_centre == 0
     quarter = lax.rem(2 * gx + gy + 2, 4)
     own = 2 * gx + gy
+    beside_y = 2 * (quarter // 2) + 1 - gy
+    beside_x = 2 * (1 - quarter // 2) + gy
     outer_start = pl.multiple_of(CENTRE_ROWS * flip, 8)
     centre_start = pl.multiple_of(OUTER_ROWS * (1 - flip), 8)
 
@@ -366,9 +368,9 @@
 
     def sample_copies(s):
         pair = 3 - gx
-        places = [(gx, y_other), (pair, gy), (pair, y_other)]
+        places = [(gx, y_other), (pair, gy)]
         if s == STEPS - 1:
-            places += [(0, gy), (0, y_other), (3, gy), (3, y_other)]
+            places += [(pair, y_other), (0, gy), (0, y_other), (3, gy), (3, y_other)]
         return [
             remote(
                 sp.at[s, quarter],
@@ -557,11 +559,14 @@
             rows.append(total)
         full[...] = jnp.concatenate(rows, axis=0)
 
+    def near_sampled(s):
+        return sp[s, quarter] + (sp[s, beside_y] + sp[s, beside_x])
+
     def sampled(s):
         return (sp[s, 0] + sp[s, 1]) + (sp[s, 2] + sp[s, 3])
 
     def force(s):
-        push = mk[10:13, :] - (full[...] if s == 0 else sampled(s)[0:3, :])
+        push = mk[10:13, :] - (full[...] if s == 0 else near_sampled(s)[0:3, :])
         spread = wx[...]
         weighted = jnp.concatenate([spread * push[c : c + 1, :] for c in range(3)], axis=0)
         body = product(weighted, wy_high[...], wy_low[...], ((1,), (1,)))
@@ -577,15 +582,15 @@
     mk_all[own] = pltpu.roll(mk_own[...], 32 * lax.rem(own, 4), 1)
 
     pl.semaphore_wait(barrier, len(neighbours))
+    for t in range(4):
+
+        @pl.when(not_self(t))
+        def _(t=t):
+            marker_copy(t).start()
+
     vouched = [neighbours[0], neighbours[1], neighbours[3]]
     for place in vouched:
         pl.semaphore_signal(vouch_sem, inc=1, device_id=place, device_id_type=MESH)
-
-    for t in range(4):
-
-        @pl.when(not_self(t))
-        def _(t=t):
-            marker_copy(t).start()
 
     for load in loads[4:]:
         load.wait()
@@ -632,8 +637,10 @@
                     copy.wait_recv()
                 sample_full()
             else:
-                for d in range(1, 4):
-                    sample_wait(s, lax.rem(quarter + d, 4))
+                sample_wait(s, beside_y)
+                sample_wait(s, beside_x)
+                if s == STEPS - 1:
+                    sample_wait(s, 3 - quarter)
             force(s)
             lax.fori_loop(OUTER_BLOCKS, BLOCKS, second_half(s), 0, unroll=True)
 

time: 46.3 us -> 46.3 us (level)
  no operation moved by 1% of the time
where the time goes in v5:
time: 46.3 us; the launch traced here: 46.1 us
  Pallas kernels  45.5 us (98%)
  between operations  0.66 us (1%)
    pallas_call x1, Pallas kernels, body(): pl.pallas_call(functools.partial(kernel, lax.axis_size('gz')), out_shape=...  44.3 us
    pallas_call x1, Pallas kernels, body(): pl.pallas_call(finish, out_shape=[jax.ShapeDtypeStruct(shape, f32) for sh...  1.15 us

profile of v5, /device:TPU:1, one launch (start us, length us, event | category | flops | bytes accessed | tf_op | source)
XLA Modules:
  0.0 46.1 jit_solution(8203366414696818796)
XLA Ops:
  0.6 0.0 copy-start
  0.6 44.3 %shard_map.85 = (f32[9,80,128]{2,1,0:T(8,128)S(1)}, f32[2,5,80,128]{3,2,1,0:T(8,128)S(1)}, f32[5,8,128]{2,1,0:T(8,128)S(1)}, f32[3,1,32]{2,1,0:T(1,128)S(1)}) custom-call(f32[19,1,64,128]{3,2,1,0:T(8,128)} %pops_in.1, s32[1,64,128]{2,1,0:T(8,128)} %solid.1, s32[2,3]{1,0:T(2,128)} %bitcast.1, s32[2,1,32]{2,1,0:T(1,128)} %cells_in.1, ...), custom_call_target="tpu_custom_call" | custom-call | flops 40000000 | bytes 2000000 | tf_op jit(solution)/shard_map/pallas_call | solution.py:722
  45.0 0.0 copy-done
  45.0 1.2 %shard_map.86 = (f32[19,1,64,128]{3,2,1,0:T(8,128)}, f32[3,1,64,128]{3,2,1,0:T(8,128)}, f32[3,1,32]{2,1,0:T(1,128)}) custom-call(f32[9,80,128]{2,1,0:T(8,128)S(1)} %get-tuple-element.7.pb, f32[2,5,80,128]{3,2,1,0:T(8,128)S(1)} %get-tuple-element.8.zr, f32[5,8,128]{2,1,0:T(8,128)S(1)} %get-tuple-element.9.er, f32[3,1,32]{2,1,0:T(1,128)S(1)} %get-tuple-element.10.force, ...), custom_call_target="tpu_custom_call" | custom-call | flops 2000000 | bytes 2000000 | tf_op jit(solution)/shard_map/pallas_call | solution.py:767
Async XLA Ops:
  0.6 44.3 %copy-start = (s32[1,64,128]{2,1,0:T(8,128)S(1)}, s32[1,64,128]{2,1,0:T(8,128)}, u32[]{:S(2)}) copy-start(s32[1,64,128]{2,1,0:T(8,128)} %solid.1) | copy-start | bytes 98308
